TPU v7x, 512 devices: a whole 4x4x16 slice. The times are simulated.
512 devices in a mesh: pipe: 16 (over y, x_hi, core), ctx: 32 (over z, x_lo).
Axes of the slice: x: 4 (x_hi: 2, x_lo: 2; x = x_hi * 2 + x_lo), y: 4, z: 16, core: 2. Of those that a mesh axis runs over, the one named last changes fastest.
Arguments:
- x_in: bfloat16 [16, 1, 5120, 2048], P('pipe', None, 'ctx'), may hold values from -6 to 6
- q_gain: float32 [16, 2048], P('pipe'), may hold values from 0.1 to 1.9
- key_gain_per_layer: float32 [16, 2048], P('pipe'), may hold values from 0.1 to 1.9
- out_gain: float32 [16, 2048], P('pipe'), may hold values from 0.1 to 1.9
- log_decay: float32 [16, 5120, 16], P('pipe', 'ctx'), may hold values from -4 to 0, as said below
- out_weight: bfloat16 [16, 2048, 2048], P('pipe', 'ctx'), may hold values from -0.125 to 0.125
Outputs:
- out: bfloat16 [16, 1, 5120, 2048], P('pipe', None, 'ctx')
Inputs may be any that keep to these rules, and one draw needn't show every extreme that they name: `log_decay`: every entry is negative.
All inputs are finite; a program needn't handle non-finite values.
Results may differ from a plain program's by a relative error of at most 0.014.
Values may be sent and summed in bfloat16 or wider, within the bound.
A program may use at most 128 MiB of HBM per device.

v0:
```python
import math

import jax
import jax.numpy as jnp
from jax import lax
from jax.sharding import PartitionSpec as P

EPS_RMS = 1e-06
TINY_NORM_GUARD = 1e-05


def carried_in(value, axis, join, neutral):
    count, mine = (lax.axis_size(axis), lax.axis_index(axis))
    pieces = jax.tree.map(lambda part: lax.all_gather(part, axis), value)
    so_far = jax.tree.map(
        lambda part, zero: jnp.full_like(part, 0) + jnp.asarray(zero, part.dtype), value, neutral
    )

    def hop(position, so_far):
        longer = join(so_far, jax.tree.map(lambda part: part[position], pieces))
        return jax.tree.map(lambda new, old: jnp.where(position < mine, new, old), longer, so_far)

    return lax.fori_loop(0, count - 1, hop, so_far)


def from_behind(value, axis, by):
    length = lax.axis_size(axis)
    return lax.ppermute(value, axis, [(i, (i + by) % length) for i in range(length)])


def rotate(values, places):
    half = values.shape[-1] // 2
    freqs = jnp.exp(
        -math.log(10000.0) * (2.0 * jnp.arange(half).astype(jnp.float32) / values.shape[-1])
    )
    angles = places[:, None] * freqs[None, :]
    cosine = jnp.cos(angles)[None, :, None, :]
    sine = jnp.sin(angles)[None, :, None, :]
    bottom_portion = values[..., :half]
    upper_half = values[..., half:]
    return jnp.concatenate(
        [bottom_portion * cosine - upper_half * sine, upper_half * cosine + bottom_portion * sine],
        axis=-1,
    )


def combine(earlier, later):
    state = later[0].astype(jnp.float32) + jnp.exp(later[1].astype(jnp.float32))[
        ..., None, None
    ] * earlier[0].astype(jnp.float32)
    total = earlier[1].astype(jnp.float32) + later[1].astype(jnp.float32)
    return (state.astype(jnp.bfloat16), total.astype(jnp.bfloat16))


def retention(x, params, offset):
    q_gain, key_gain_per_layer, out_gain, log_decay = params
    micro, rows, width = x.shape
    heads = log_decay.shape[-1]
    size = width // heads
    floats = x.astype(jnp.float32)
    normed = floats * lax.rsqrt(jnp.mean(floats * floats, axis=-1, keepdims=True) + EPS_RMS)
    places = (offset + jnp.arange(rows, dtype=jnp.int32)).astype(jnp.float32)
    query = rotate((normed * q_gain).reshape(micro, rows, heads, size), places).astype(jnp.bfloat16)
    key_rot = rotate(
        (normed * key_gain_per_layer).reshape(micro, rows, heads, size), places
    ).astype(jnp.bfloat16)
    value = normed.reshape(micro, rows, heads, size).astype(jnp.bfloat16)
    running = jnp.cumsum(log_decay, axis=0)
    scores = jnp.einsum("mnhd,mkhd->mhnk", query, key_rot, preferred_element_type=jnp.float32)
    lower = jnp.arange(rows)[:, None] >= jnp.arange(rows)[None, :]
    across = running.T
    dispersion_width = across[:, :, None] - across[:, None, :]
    weight = jnp.exp(jnp.where(lower[None], dispersion_width, -1e30))
    probs = (scores * weight[None]).astype(jnp.bfloat16)
    inner = jnp.einsum("mhnk,mkhd->mnhd", probs, value, preferred_element_type=jnp.float32)
    final_run = running[-1]
    shrunk = (key_rot * jnp.exp(final_run[None, :] - running)[None, :, :, None]).astype(
        jnp.bfloat16
    )
    local_shard_state = jnp.einsum(
        "mkhd,mkhe->mhde", shrunk, value, preferred_element_type=jnp.float32
    ).astype(jnp.bfloat16)
    total = final_run[None, :].astype(jnp.bfloat16)
    entering, _ = carried_in(
        (local_shard_state, total),
        "ctx",
        combine,
        (jnp.zeros_like(local_shard_state), jnp.zeros_like(total)),
    )
    carried = jnp.einsum("mnhd,mhde->mnhe", query, entering, preferred_element_type=jnp.float32)
    mixed = inner + carried * jnp.exp(running)[None, :, :, None]
    centre = mixed - jnp.mean(mixed, axis=-1, keepdims=True)
    normal = centre * lax.rsqrt(jnp.mean(centre * centre, axis=-1, keepdims=True) + TINY_NORM_GUARD)
    scaled = (normal.reshape(micro, rows, width) * out_gain).astype(jnp.bfloat16)
    return (floats, scaled.reshape(micro * rows, width))


def per_device(x_in, q_gain, key_gain_per_layer, out_gain, log_decay, out_weight):
    offset = lax.axis_index("ctx") * x_in.shape[2]
    own_params = (q_gain[0], key_gain_per_layer[0], out_gain[0], log_decay[0])
    floats, scaled = retention(x_in[0], own_params, offset)
    whole_weight = lax.all_gather(out_weight[0], "ctx", axis=0, tiled=True)
    product = jnp.dot(scaled, whole_weight, preferred_element_type=jnp.float32)
    first = (floats + product.reshape(floats.shape)).astype(jnp.bfloat16)
    moved = from_behind(first, "pipe", 1)
    return moved[None]


def solution(mesh):
    placed = (
        P("pipe", None, "ctx", None),
        P("pipe", None),
        P("pipe", None),
        P("pipe", None),
        P("pipe", "ctx", None),
        P("pipe", "ctx", None),
    )
    return jax.shard_map(
        per_device,
        mesh=mesh,
        in_specs=placed,
        out_specs=P("pipe", None, "ctx", None),
        check_vma=False,
    )
```

profile of v0, /device:TPU:2, one launch (start us, length us, event | category | flops | bytes accessed | tf_op | source)
XLA Modules:
  0.0 617.2 jit_solution(11407001303944431956)
XLA Ops:
  13.8 2.4 convolution_convert_fusion
  17.1 72.0 %all-gather.3 = bf16[32,1,16]{2,1,0:T(2,128)(2,1)S(1)} all-gather(bf16[1,1,16]{2,1,0:T(2,128)(2,1)S(1)} %bitcast.102), channel_id=3, replica_groups=mesh['pipe'=16,'ctx'=32] {'ctx'}, dimensions={0}, use_global_device_ids=true | all-gather | bytes 1056 | tf_op jit(solution)/shard_map/all_gather | solution.py:14
  89.2 4.4 convolution_bitcast_fusion
  93.5 294.5 %all-gather.7.cloned.1.call-done = bf16[512,128,128]{2,1,0:T(8,128)(2,1)} async-done(((bf16[16,128,128]{2,1,0:T(8,128)(2,1)}), bf16[512,128,128]{2,1,0:T(8,128)(2,1)}) %all-gather.7.cloned.1.call-update) | async-done | bytes 16777232 | tf_op jit(solution)/shard_map/all_gather | solution.py:14
  388.0 45.1 %while.14 = (s32[]{:T(128)}, bf16[1,16,128,128]{3,2,1,0:T(8,128)(2,1)S(1)}, s32[]{:T(128)}, bf16[32,1,16,128,128]{4,3,2,1,0:T(8,128)(2,1)}, bf16[32,1,16]{2,1,0:T(2,128)(2,1)S(1)}, /*index=5*/s32[]{:T(128)}, s32[]{:T(128)}) while((s32[]{:T(128)}, bf16[1,16,128,128]{3,2,1,0:T(8,128)(2,1)S(1)}, s32[]{:T(128)}, ...), condition=%wide.region_4.5_spmd.clone, body=%wide.region_3.4_spmd.clone.sunk | while | flops 1835028 | bytes 1573129 | solution.py:23
  388.0 1.5 fusion.38
  391.0 1.4 fusion.38
  392.5 1.4 fusion.38
  393.9 1.4 fusion.38
  395.4 1.4 fusion.38
  396.8 1.4 fusion.38
  398.3 1.4 fusion.38
  399.7 1.4 fusion.38
  401.2 1.4 fusion.38
  402.6 1.4 fusion.38
  404.1 1.4 fusion.38
  415.7 1.4 fusion.38
  420.1 1.4 fusion.38
  423.0 1.4 fusion.38
  427.3 1.4 fusion.38
  437.1 151.7 %all-gather.9.cloned.1.call-done = bf16[1,2048,2048]{2,1,0:T(8,128)(2,1)} async-done(((bf16[1,64,2048]{2,1,0:T(8,128)(2,1)}), bf16[1,2048,2048]{2,1,0:T(8,128)(2,1)}) %all-gather.9.cloned.1.call-update) | async-done | bytes 8388624 | tf_op jit(solution)/shard_map/all_gather | solution.py:102
  588.9 5.1 fusion.10
  594.0 1.9 collective-permute-start
  595.9 13.6 %collective-permute-done = bf16[1,160,2048]{2,1,0:T(8,128)(2,1)S(1)} collective-permute-done((bf16[1,160,2048]{2,1,0:T(8,128)(2,1)S(1)}, bf16[1,160,2048]{2,1,0:T(8,128)(2,1)S(1)}, u32[]{:S(2)}, u32[]{:S(2)}) %collective-permute-start) | collective-permute-done | bytes 655392 | tf_op jit(solution)/shard_map/ppermute | solution.py:28
  (94 shorter events, 35.7 us)
Async XLA Ops:
  6.5 381.5 %all-gather.7.cloned.1.call-start = ((), (), s32[]{:S(2)}) async-start(), calls=%async_computation | async-start | bytes 17301504 | tf_op jit(solution)/shard_map/all_gather | solution.py:14
  9.1 0.7 copy-start.5
  9.1 2.2 copy-start.6
  9.1 2.2 copy-start.7
  12.7 0.8 copy-start.1
  12.7 1.0 copy-start.2
  16.2 572.7 %all-gather.9.cloned.1.call-start = ((), (), s32[]{:S(2)}) async-start(), calls=%async_computation.1 | async-start | bytes 8650752 | tf_op jit(solution)/shard_map/all_gather | solution.py:102
  388.0 45.1 %copy-start.3 = (f32[1,160,16,128]{3,1,2,0:T(8,128)S(1)}, f32[1,160,16,128]{3,1,2,0:T(8,128)}, u32[]{:S(2)}) copy-start(f32[1,160,16,128]{3,1,2,0:T(8,128)} %convolution_bitcast_fusion) | copy-start | bytes 3932164
  436.3 152.5 %copy-start = (bf16[1,1,160,2048]{3,2,1,0:T(8,128)(2,1)S(1)}, bf16[1,1,160,2048]{3,2,1,0:T(8,128)(2,1)}, u32[]{:S(2)}) copy-start(bf16[1,1,160,2048]{3,2,1,0:T(8,128)(2,1)} %param.8) | copy-start | bytes 1966084
  436.3 152.5 %copy-start.4 = (f32[1,2048]{1,0:T(1,128)S(1)}, f32[1,2048]{1,0:T(1,128)}, u32[]{:S(2)}) copy-start(f32[1,2048]{1,0:T(1,128)} %param.11) | copy-start | bytes 24580
  594.0 15.5 %collective-permute-start = (bf16[1,160,2048]{2,1,0:T(8,128)(2,1)S(1)}, bf16[1,160,2048]{2,1,0:T(8,128)(2,1)S(1)}, u32[]{:S(2)}, u32[]{:S(2)}) collective-permute-start(bf16[1,160,2048]{2,1,0:T(8,128)(2,1)S(1)} %fusion.10), channel_id=1, source_target_pairs={{0,32},{32,64},{64,96},{96,128},{128,160},{160,192},{192,224},{224... | collective-permute-start | bytes 1966088 | tf_op jit(solution)/shard_map/ppermute | solution.py:28
Sparse Core Ops, SparseCore 0:
  16.3 371.6 all-gather.6
  390.1 198.7 all-gather.8
where the time goes:
time: 619 us; the launch traced here: 617 us
  waiting for transfers between devices  461 us (74%)
  blocking collectives  72 us (12%)
  other arithmetic  51 us (8%)
  between operations  13.6 us (2%)
  matrix products  13.2 us (2%)
    all_gather x1, waiting for transfers between devices, carried_in(): pieces = jax.tree.map(lambda part: lax.all_gather(part, axis), value)  294 us
    all_gather x1, waiting for transfers between devices, per_device(): whole_weight = lax.all_gather(out_weight[0], 'ctx', axis=0, tiled=True)  152 us
    all_gather x1, blocking collectives, carried_in(): pieces = jax.tree.map(lambda part: lax.all_gather(part, axis), value)  72 us
    select_n x31, other arithmetic, hop(): jnp.where(position < mine, new, old)  43.8 us
    ppermute x1, waiting for transfers between devices, from_behind(): lax.ppermute(value, axis, [(i, (i + by) % length) for i in range(length)])  13.6 us
  transfers between devices with their start and end apart: 3, of which 3 were waited for; matrix products, arithmetic and copies ran while one was open for 9% of the time, Pallas kernels for 0%

commit v1 on v0

v1 whole, which is shorter than its diff:
```python
import jax
import jax.numpy as jnp
import numpy as np
from jax import lax
from jax.experimental import pallas as pl
from jax.experimental.pallas import tpu as pltpu
from jax.sharding import PartitionSpec as P

EPS_RMS = 1e-06
EPS_NORM = 1e-05
MESH = pl.DeviceIdType.MESH
BF, F32 = jnp.bfloat16, jnp.float32
ROWS, WIDTH, HALF, HEAD, HEADS, OWN = 160, 2048, 1024, 128, 16, 8
Z, SUBS, PARTS, COLS = 16, 4, 4, 256
SUB = 128 // SUBS


def tables():
    freqs = 10000.0 ** (-2.0 * np.arange(64) / 128.0)
    freqs = np.concatenate([freqs, freqs])[None, :]
    sign = np.where(np.arange(128) < 64, -1.0, 1.0)[None, :]
    coarse = np.arange(32)[:, None] * float(ROWS) * freqs
    fine = np.arange(ROWS)[:, None] * freqs
    return tuple(
        np.stack([np.cos(a), sign * np.sin(a), np.sin(a)]).astype(np.float32) for a in (coarse, fine)
    )


def remote(src, dst, send, recv, device):
    return pltpu.make_async_remote_copy(
        src_ref=src, dst_ref=dst, send_sem=send, recv_sem=recv, device_id=device, device_id_type=MESH
    )


def dot(a, b, dims=((1,), (0,)), precision=None):
    return lax.dot_general(a, b, (dims, ((), ())), precision=precision, preferred_element_type=F32)


def kernel(
    x_ref, qg_ref, kg_ref, og_ref, ld_ref, w_ref, coarse_ref, fine_ref,
    out_ref,
    xh, iv, ldh, rb, rt, cs, sn, kb, vb, qb, st, inner, zs, zr, eo, ei, wz, act, ost,
    is_, ir, ws, wr, z1s, z1r, z2s, z2r, as_, ar, os_, or_,
):
    pipe, ctx = lax.axis_index("pipe"), lax.axis_index("ctx")
    z, x = ctx // 2, lax.rem(ctx, 2)
    y = 1 - x
    mate = {"ctx": 2 * z + y}
    following, before = lax.rem(pipe + 1, 16), lax.rem(pipe + 15, 16)
    mine = pl.multiple_of(x * HALF, HALF)
    theirs = pl.multiple_of(y * HALF, HALF)

    def level(d):
        return lax.rem(z + d, Z)

    def at_level(zz):
        return {"ctx": 2 * zz + x}

    barrier = pltpu.get_barrier_semaphore()

    def greet(d, carry):
        pl.semaphore_signal(barrier, inc=1, device_id=at_level(level(d)), device_id_type=MESH)
        return carry

    pl.semaphore_signal(barrier, inc=1, device_id=mate, device_id_type=MESH)
    lax.fori_loop(1, Z, greet, 0)
    for b in range(2):
        for p in (following, before):
            pl.semaphore_signal(
                barrier, inc=1, device_id={"pipe": p, "ctx": 2 * z + b}, device_id_type=MESH
            )

    floats = x_ref[...].astype(F32)
    scale = lax.rsqrt(jnp.mean(floats * floats, axis=-1, keepdims=True) + EPS_RMS)
    iv[x] = jnp.broadcast_to(scale, (ROWS, HEAD))
    xh[x] = x_ref[:, pl.ds(mine, HALF)]
    ldh[x] = ld_ref[pl.ds(pl.multiple_of(x * OWN, OWN), OWN), :]
    wz[z, pl.ds(pl.multiple_of(x * 64, 64), 64)] = w_ref[:, pl.ds(mine, HALF)]

    pl.semaphore_wait(barrier, Z + 4)

    first = [
        remote(x_ref.at[:, pl.ds(theirs, HALF)], xh.at[x], is_.at[0], ir.at[0], mate),
        remote(
            ld_ref.at[pl.ds(pl.multiple_of(y * OWN, OWN), OWN)], ldh.at[x], is_.at[1], ir.at[1], mate
        ),
        remote(iv.at[x], iv.at[x], is_.at[2], ir.at[2], mate),
        remote(
            w_ref.at[:, pl.ds(theirs, HALF)],
            wz.at[z, pl.ds(pl.multiple_of(x * 64, 64), 64)],
            is_.at[3], ir.at[3], mate,
        ),
    ]
    for i in (3, 1, 2, 0):
        first[i].start()

    def ring_copy(way, step, u):
        block = level(Z - step) if way == 0 else level(step)
        rows = pl.ds(u * SUB, SUB)
        return remote(
            wz.at[block, rows], wz.at[block, rows], ws.at[way, step, u], wr.at[way, step, u],
            at_level(level(1 if way == 0 else Z - 1)),
        )

    def used(way, step, u):
        return step < 7 or (u < SUBS // 2) == (way == 0)

    def arrived(way, step, u):
        block = level(Z - 1 - step) if way == 0 else level(step + 1)
        rows = pl.ds(u * SUB, SUB)
        remote(
            wz.at[block, rows], wz.at[block, rows], ws.at[way, step, u], wr.at[way, step, u],
            at_level(level(1)),
        ).wait_recv()

    def serve(step):
        for u in range(SUBS):
            for way in range(2):
                if step > 0 and used(way, step - 1, u):
                    arrived(way, step - 1, u)
                if step < 8 and used(way, step, u):
                    ring_copy(way, step, u).start()

    for b in range(2):
        row = pl.ds(2 * z + b, 1)
        ca, sa, su = coarse_ref[0, row], coarse_ref[1, row], coarse_ref[2, row]
        cs[b] = ca * fine_ref[0] - su * fine_ref[2]
        sn[b] = sa * fine_ref[0] + ca * fine_ref[1]
    rows_i = lax.broadcasted_iota(jnp.int32, (ROWS, ROWS), 0)
    cols_i = lax.broadcasted_iota(jnp.int32, (ROWS, ROWS), 1)
    lower = rows_i >= cols_i

    first[3].wait_recv()
    serve(0)
    first[1].wait_recv()
    lower_f = lower.astype(F32)
    for b in range(2):
        lds = ldh[b]
        rt[b] = dot(lds, lower_f, ((1,), (1,)), lax.Precision.HIGHEST)
        run = dot(lower_f, lds, ((1,), (1,)), lax.Precision.HIGHEST)
        for h in range(OWN):
            rb[b, h] = jnp.broadcast_to(run[:, h : h + 1], (ROWS, HEAD))
    first[2].wait_recv()
    first[0].wait_recv()

    def lanes(h):
        return pl.ds(pl.multiple_of(h * HEAD, HEAD), HEAD)

    def gain_of(ref, h):
        return ref[:, pl.ds(pl.multiple_of(x * HALF + h * HEAD, HEAD), HEAD)]

    def normed_of(b, h):
        return xh[b, :, lanes(h)].astype(F32) * iv[b]

    def rotated(u, b):
        return (u * cs[b] + pltpu.roll(u, 64, axis=1) * sn[b]).astype(BF)

    def last_of(b, h):
        return rb[b, h, ROWS - 1 : ROWS, :]

    def total_of(b, h):
        return last_of(b, h).astype(BF).astype(F32)

    def states(h, carry):
        made = []
        for b in range(2):
            normed = normed_of(b, h)
            value = normed.astype(BF)
            key = rotated(normed * gain_of(kg_ref, h), b)
            kb[b, h] = key
            vb[b, h] = value
            shrunk = (key.astype(F32) * jnp.exp(last_of(b, h) - rb[b, h])).astype(BF)
            state = dot(shrunk, value, ((0,), (0,))).astype(BF)
            made.append(state.astype(F32))
        st[h] = made[0].astype(BF)
        early, late = total_of(0, h), total_of(1, h)
        pair = (made[1] + jnp.exp(late) * made[0]).astype(BF)
        sums = jnp.concatenate(
            [jnp.broadcast_to(early, (8, HEAD)), jnp.broadcast_to(late, (8, HEAD))], axis=0
        ).astype(BF)
        for half in range(2):
            zs[2 * h + half, 0:64, :] = pair[half * 64 : half * 64 + 64]
            zs[2 * h + half, 64:80, :] = sums
        return carry

    lax.fori_loop(0, OWN // 2, states, 0)
    serve(1)
    lax.fori_loop(OWN // 2, OWN, states, 0)

    def send_pairs(d, carry):
        zz = level(d)
        remote(zs.at[zz], zr.at[z], z1s.at[zz], z1r.at[z], at_level(zz)).start()
        return carry

    lax.fori_loop(1, Z, send_pairs, 0)
    zr[z] = zs[z]

    def inside(h, carry):
        for b in range(2):
            query = rotated(normed_of(b, h) * gain_of(qg_ref, h), b)
            qb[b, h] = query
            scores = dot(query, kb[b, h], ((1,), (1,)))
            spread = rb[b, h, :, 0:1] - rt[b, pl.ds(h, 1), :]
            weight = jnp.exp(jnp.where(lower, spread, -1e30))
            inner[b, h] = dot((scores * weight).astype(BF), vb[b, h])
        return carry

    lax.fori_loop(0, OWN // 2, inside, 0)
    serve(2)
    lax.fori_loop(OWN // 2, OWN, inside, 0)
    serve(3)

    def scan(zz, state):
        @pl.when(zz != z)
        def _():
            remote(zs.at[zz], zr.at[zz], z1s.at[zz], z1r.at[zz], at_level(zz)).wait_recv()

        eo[zz] = state.astype(BF)

        @pl.when(zz != z)
        def _():
            remote(eo.at[zz], ei.at[z], z2s.at[zz], z2r.at[z], at_level(zz)).start()

        sums = zr[zz, 64:80, :].astype(F32)
        decay = jnp.exp(sums[0:1] + sums[8:9])
        return zr[zz, 0:64, :].astype(F32) + decay * state

    lax.fori_loop(0, Z, scan, jnp.zeros((64, HEAD), F32))
    ei[z] = eo[z]
    serve(4)
    serve(5)

    def head_copy(h):
        g = x * OWN + h
        slot = act.at[g // 2, :, lanes(lax.rem(g, 2))]
        return remote(slot, slot, as_.at[h], ar.at[h], mate)

    def finish(h, carry):
        for half in range(2):
            zz = 2 * h + half

            @pl.when(zz != z)
            def _():
                remote(eo.at[zz], ei.at[zz], z2s.at[zz], z2r.at[zz], at_level(zz)).wait_recv()

        entering = jnp.concatenate([ei[2 * h], ei[2 * h + 1]], axis=0)
        after = (st[h].astype(F32) + jnp.exp(total_of(0, h)) * entering.astype(F32)).astype(BF)
        g = x * OWN + h
        for b in range(2):
            carried = dot(qb[b, h], entering if b == 0 else after)
            mixed = inner[b, h] + carried * jnp.exp(rb[b, h])
            centre = mixed - jnp.mean(mixed, axis=-1, keepdims=True)
            normal = centre * lax.rsqrt(
                jnp.mean(centre * centre, axis=-1, keepdims=True) + EPS_NORM
            )
            act[g // 2, b * ROWS : (b + 1) * ROWS, lanes(lax.rem(g, 2))] = (
                normal * gain_of(og_ref, h)
            ).astype(BF)
        head_copy(h).start()
        return carry

    lax.fori_loop(0, OWN, finish, 0)
    serve(6)
    serve(7)
    serve(8)

    def partner_head(h, carry):
        g = y * OWN + h
        slot = act.at[g // 2, :, lanes(lax.rem(g, 2))]
        remote(slot, slot, as_.at[h], ar.at[h], mate).wait_recv()
        return carry

    lax.fori_loop(0, OWN, partner_head, 0)

    def out_copy(b, n):
        place = pl.ds(pl.multiple_of(x * HALF + n * COLS, COLS), COLS)
        return remote(
            ost.at[b, :, pl.ds(n * COLS, COLS)], out_ref.at[:, place],
            os_.at[b, n], or_.at[x, n], {"pipe": following, "ctx": 2 * z + b},
        )

    for n in range(PARTS):
        here = slice(n * COLS, (n + 1) * COLS)
        total = jnp.zeros((2 * ROWS, COLS), F32)
        for j in range(Z // 2):
            block = jnp.concatenate([wz[2 * j, :, here], wz[2 * j + 1, :, here]], axis=0)
            total = total + dot(act[j], block)
        for b in range(2):
            ost[b, :, here] = (
                xh[b, :, here].astype(F32) + total[b * ROWS : (b + 1) * ROWS]
            ).astype(BF)
            out_copy(b, n).start()

    for half in range(2):
        for n in range(PARTS):
            remote(
                ost.at[0, :, pl.ds(n * COLS, COLS)],
                out_ref.at[:, pl.ds(half * HALF + n * COLS, COLS)],
                os_.at[0, n], or_.at[half, n], mate,
            ).wait_recv()
    for b in range(2):
        for n in range(PARTS):
            out_copy(b, n).wait_send()
    for copy in first:
        copy.wait_send()
    for step in range(8):
        for u in range(SUBS):
            for way in range(2):
                if used(way, step, u):
                    ring_copy(way, step, u).wait_send()

    def sent(d, carry):
        zz = level(d)
        remote(zs.at[zz], zr.at[z], z1s.at[zz], z1r.at[z], at_level(zz)).wait_send()
        remote(eo.at[zz], ei.at[z], z2s.at[zz], z2r.at[z], at_level(zz)).wait_send()
        return carry

    lax.fori_loop(1, Z, sent, 0)

    def head_sent(h, carry):
        head_copy(h).wait_send()
        return carry

    lax.fori_loop(0, OWN, head_sent, 0)


def per_device(x_in, q_gain, key_gain_per_layer, out_gain, log_decay, out_weight):
    coarse, fine = (jnp.asarray(t) for t in tables())
    dma = pltpu.SemaphoreType.DMA
    vmem = pltpu.VMEM
    scratch = [
        vmem((2, ROWS, HALF), BF),
        vmem((2, ROWS, HEAD), F32),
        vmem((2, OWN, ROWS), F32),
        vmem((2, OWN, ROWS, HEAD), F32),
        vmem((2, OWN, ROWS), F32),
        vmem((2, ROWS, HEAD), F32),
        vmem((2, ROWS, HEAD), F32),
        vmem((2, OWN, ROWS, HEAD), BF),
        vmem((2, OWN, ROWS, HEAD), BF),
        vmem((2, OWN, ROWS, HEAD), BF),
        vmem((OWN, HEAD, HEAD), BF),
        vmem((2, OWN, ROWS, HEAD), F32),
        vmem((Z, 80, HEAD), BF),
        vmem((Z, 80, HEAD), BF),
        vmem((Z, 64, HEAD), BF),
        vmem((Z, 64, HEAD), BF),
        vmem((Z, 128, HALF), BF),
        vmem((Z // 2, 2 * ROWS, 2 * HEAD), BF),
        vmem((2, ROWS, HALF), BF),
        dma((4,)), dma((4,)),
        dma((2, 8, SUBS)), dma((2, 8, SUBS)),
        dma((Z,)), dma((Z,)), dma((Z,)), dma((Z,)),
        dma((OWN,)), dma((OWN,)),
        dma((2, PARTS)), dma((2, PARTS)),
    ]
    whole = pl.BlockSpec(memory_space=pltpu.VMEM)
    out = pl.pallas_call(
        kernel,
        out_shape=jax.ShapeDtypeStruct((ROWS, WIDTH), BF),
        in_specs=[whole] * 8,
        out_specs=whole,
        scratch_shapes=scratch,
        compiler_params=pltpu.CompilerParams(
            collective_id=0, has_side_effects=True, vmem_limit_bytes=48 * 2**20
        ),
        name="retention_layer",
    )(
        x_in[0, 0], q_gain, key_gain_per_layer, out_gain, log_decay[0].T, out_weight[0], coarse, fine
    )
    return out[None, None]


def solution(mesh):
    placed = (
        P("pipe", None, "ctx", None),
        P("pipe", None),
        P("pipe", None),
        P("pipe", None),
        P("pipe", "ctx", None),
        P("pipe", "ctx", None),
    )
    return jax.shard_map(
        per_device,
        mesh=mesh,
        in_specs=placed,
        out_specs=P("pipe", None, "ctx", None),
        check_vma=False,
    )
```

time: 619 us -> 114 us (0.18)
  waiting for transfers between devices: 461 us -> 0 us
  Pallas kernels: 0 us -> 106 us
  blocking collectives: 72 us -> 0 us
  other arithmetic: 51 us -> 0 us
  between operations: 13.6 us -> 0.02 us
  matrix products: 13.2 us -> 0 us
    all_gather x2 -> x0, waiting for transfers between devices: 446 us -> none  [the longest x1 294 us: carried_in(): pieces = jax.tree.map(lambda part: lax.all_gather(part, axis), value)]
    pallas_call x0 -> x1, Pallas kernels: none -> 106 us  [per_device(): pl.pallas_call(kernel, out_shape=jax.ShapeDtypeStruct((ROWS, WIDTH), BF),...]
    all_gather x1 -> x0, blocking collectives: 72 us -> none  [carried_in(): pieces = jax.tree.map(lambda part: lax.all_gather(part, axis), value)]
    select_n x31 -> x0, other arithmetic: 43.8 us -> none  [hop(): jnp.where(position < mine, new, old)]
    ppermute x1 -> x0, waiting for transfers between devices: 13.6 us -> none  [from_behind(): lax.ppermute(value, axis, [(i, (i + by) % length) for i in range(length)])]
    dot_general x4 -> x0, matrix products: 13.2 us -> none  [the longest x1 5.15 us: per_device(): product = jnp.dot(scaled, whole_weight, preferred_element_type=jnp.float32)]
  transfers between devices with their start and end apart: 3 -> 0, of which waited for: 3 -> 0; matrix products, arithmetic and copies ran while one was open for 9% -> 0% of each run, Pallas kernels for 0% -> 0%
where the time goes in v1:
time: 114 us; the launch traced here: 113 us
  Pallas kernels  106 us (93%)
  local copies, waits for them, and re-layouts  7.42 us (7%)
    pallas_call x1, Pallas kernels, per_device(): pl.pallas_call(kernel, out_shape=jax.ShapeDtypeStruct((ROWS, WIDTH), BF),...  106 us
    unnamed x17, local copies, waits for them, and re-layouts  7.42 us

profile of v1, /device:TPU:2, one launch (start us, length us, event | category | flops | bytes accessed | tf_op | source)
XLA Modules:
  0.0 113.3 jit_solution(12631753288402122397)
XLA Ops:
  0.0 0.0 copy-start
  0.0 1.1 copy-done
  1.1 0.0 copy-start.1
  1.1 0.9 copy-done.1
  2.0 0.0 copy-start.2
  2.0 0.9 copy-done.2
  3.0 0.0 copy-start.3
  3.0 0.8 copy-done.3
  3.8 0.0 copy-start.4
  3.8 0.7 copy-done.4
  4.5 0.0 copy-start.5
  4.5 0.7 copy-done.5
  5.2 0.0 copy-start.6
  5.2 0.7 copy-done.6
  5.9 0.0 copy-start.7
  5.9 0.7 copy-done.7
  6.6 105.8 %retention_layer.1 = bf16[160,2048]{1,0:T(8,128)(2,1)S(1)} custom-call(bf16[160,2048]{1,0:T(8,128)(2,1)S(1)} %bitcast.7, f32[1,2048]{1,0:T(1,128)S(1)} %copy-done.5, f32[1,2048]{1,0:T(1,128)S(1)} %copy-done.6, f32[1,2048]{1,0:T(1,128)S(1)} %copy-done.7, f32[16,160]{1,0:T(8,128)S(1)} %bitcast.9, bf16[64,2048]{1,0:T(8,128)(2,1)S(1)} %bitcast.8, ...), custom_call_target="tpu_custom_call" | custom-call | tf_op jit(solution)/shard_map/retention_layer/pallas_call | solution.py:358
  112.4 0.8 copy.10
Async XLA Ops:
  0.0 1.1 copy-start
  1.1 0.9 copy-start.1
  2.0 0.9 copy-start.2
  3.0 0.8 copy-start.3
  3.8 0.7 copy-start.4
  4.5 0.7 copy-start.5
  5.2 0.7 copy-start.6
  5.9 0.7 copy-start.7

commit v2 on v1

v2 whole, which is shorter than its diff:
```python
import jax
import jax.numpy as jnp
import numpy as np
from jax import lax
from jax.experimental import pallas as pl
from jax.experimental.pallas import tpu as pltpu
from jax.sharding import PartitionSpec as P

EPS_RMS = 1e-06
EPS_NORM = 1e-05
MESH = pl.DeviceIdType.MESH
BF, F32 = jnp.bfloat16, jnp.float32
ROWS, WIDTH, HALF, HEAD, HEADS, OWN = 160, 2048, 1024, 128, 16, 8
Z, QUAD, SUBS, PARTS, COLS = 16, 4, 4, 4, 256
SUB = 128 // SUBS


def tables():
    freqs = 10000.0 ** (-2.0 * np.arange(64) / 128.0)
    freqs = np.concatenate([freqs, freqs])[None, :]
    sign = np.where(np.arange(128) < 64, -1.0, 1.0)[None, :]
    coarse = np.arange(32)[:, None] * float(ROWS) * freqs
    fine = np.arange(ROWS)[:, None] * freqs
    return tuple(
        np.stack([np.cos(a), sign * np.sin(a), np.sin(a)]).astype(np.float32) for a in (coarse, fine)
    )


def remote(src, dst, send, recv, device):
    return pltpu.make_async_remote_copy(
        src_ref=src, dst_ref=dst, send_sem=send, recv_sem=recv, device_id=device, device_id_type=MESH
    )


def dot(a, b, dims=((1,), (0,)), precision=None):
    return lax.dot_general(a, b, (dims, ((), ())), precision=precision, preferred_element_type=F32)


def kernel(
    x_hbm, qg_hbm, kg_hbm, og_hbm, ld_hbm, w_hbm, coarse_hbm, fine_hbm,
    out_ref,
    xv, gains, ldv, coarse, fine,
    xh, iv, ldh, rb, rt, cs, sn, kb, vb, qb, st, inner, zs, zr, gs, gr, eo, er, fo, ei, wz, act, acc, ost,
    ins, is_, ir, ws, wr, s1, r1, s2, r2, s3, r3, s4, r4, as_, ar, os_, or_,
):
    pipe, ctx = lax.axis_index("pipe"), lax.axis_index("ctx")
    z, x = ctx // 2, lax.rem(ctx, 2)
    quad, place = z // QUAD, lax.rem(z, QUAD)
    y = 1 - x
    mate = {"ctx": 2 * z + y}
    following, before = lax.rem(pipe + 1, 16), lax.rem(pipe + 15, 16)
    mine = pl.ds(pl.multiple_of(x * HALF, HALF), HALF)
    theirs = pl.ds(pl.multiple_of(y * HALF, HALF), HALF)

    def level(d):
        return lax.rem(z + d, Z)

    def at_level(zz):
        return {"ctx": 2 * zz + x}

    def at_place(p):
        return at_level(quad * QUAD + p)

    def at_quad(q):
        return at_level(q * QUAD + place)

    barrier = pltpu.get_barrier_semaphore()
    greeted = [mate, at_level(level(1)), at_level(level(Z - 1))]
    for d in range(1, QUAD):
        greeted.append(at_place(lax.rem(place + d, QUAD)))
        greeted.append(at_quad(lax.rem(quad + d, QUAD)))
    for b in range(2):
        for p in (following, before):
            greeted.append({"pipe": p, "ctx": 2 * z + b})
    for device in greeted:
        pl.semaphore_signal(barrier, inc=1, device_id=device, device_id_type=MESH)

    own_rows = pl.ds(pl.multiple_of(x * 64, 64), 64)
    fetches = [
        pltpu.make_async_copy(w_hbm.at[:, mine], wz.at[z, own_rows], ins.at[0]),
        pltpu.make_async_copy(x_hbm, xv, ins.at[1]),
        pltpu.make_async_copy(ld_hbm, ldv, ins.at[2]),
        pltpu.make_async_copy(coarse_hbm, coarse, ins.at[3]),
        pltpu.make_async_copy(fine_hbm, fine, ins.at[4]),
        pltpu.make_async_copy(kg_hbm.at[:, mine], gains.at[0], ins.at[5]),
        pltpu.make_async_copy(qg_hbm.at[:, mine], gains.at[1], ins.at[6]),
        pltpu.make_async_copy(og_hbm.at[:, mine], gains.at[2], ins.at[7]),
    ]
    for fetch in fetches:
        fetch.start()

    fetches[1].wait()
    floats = xv[...].astype(F32)
    scale = lax.rsqrt(jnp.mean(floats * floats, axis=-1, keepdims=True) + EPS_RMS)
    iv[x] = jnp.broadcast_to(scale, (ROWS, HEAD))
    xh[x] = xv[:, mine]
    fetches[2].wait()
    ldh[x] = ldv[pl.ds(pl.multiple_of(x * OWN, OWN), OWN), :]
    fetches[0].wait()

    pl.semaphore_wait(barrier, len(greeted))

    def ring_copy(way, step, k, came):
        block = level(Z - step - came) if way == 0 else level(step + came)
        rows = pl.ds(pl.multiple_of(lax.rem(2 * x + k, SUBS) * SUB, SUB), SUB)
        return remote(
            wz.at[block, rows], wz.at[block, rows], ws.at[way, step, k], wr.at[way, step, k],
            at_level(level(1 if way == 0 else Z - 1)),
        )

    def used(way, step, k):
        return step < 7 or (k < SUBS // 2) == (way == 0)

    def serve(step, parts=range(SUBS)):
        for k in parts:
            for way in range(2):
                if step > 0 and used(way, step - 1, k):
                    ring_copy(way, step - 1, k, 1).wait_recv()
                if step < 8 and used(way, step, k):
                    ring_copy(way, step, k, 0).start()

    first = [
        remote(w_hbm.at[:, theirs], wz.at[z, own_rows], is_.at[0], ir.at[0], mate),
        remote(
            ldv.at[pl.ds(pl.multiple_of(y * OWN, OWN), OWN)], ldh.at[x], is_.at[1], ir.at[1], mate
        ),
        remote(iv.at[x], iv.at[x], is_.at[2], ir.at[2], mate),
        remote(xv.at[:, theirs], xh.at[x], is_.at[3], ir.at[3], mate),
    ]
    first[0].start()
    serve(0, (0, 1))
    for copy in first[1:]:
        copy.start()

    fetches[3].wait()
    fetches[4].wait()
    for b in range(2):
        row = pl.ds(2 * z + b, 1)
        ca, sa, su = coarse[0, row], coarse[1, row], coarse[2, row]
        cs[b] = ca * fine[0] - su * fine[2]
        sn[b] = sa * fine[0] + ca * fine[1]
    rows_i = lax.broadcasted_iota(jnp.int32, (ROWS, ROWS), 0)
    cols_i = lax.broadcasted_iota(jnp.int32, (ROWS, ROWS), 1)
    lower = rows_i >= cols_i
    lower_f = lower.astype(F32)
    for i in (5, 6, 7):
        fetches[i].wait()

    first[0].wait_recv()
    serve(0, (2, 3))
    first[1].wait_recv()
    for b in range(2):
        lds = ldh[b]
        rt[b] = dot(lds, lower_f, ((1,), (1,)), lax.Precision.HIGHEST)
        run = dot(lower_f, lds, ((1,), (1,)), lax.Precision.HIGHEST)
        for h in range(OWN):
            rb[b, h] = jnp.broadcast_to(run[:, h : h + 1], (ROWS, HEAD))
    first[2].wait_recv()
    first[3].wait_recv()

    def lanes(h):
        return pl.ds(pl.multiple_of(h * HEAD, HEAD), HEAD)

    def normed_of(b, h):
        return xh[b, :, lanes(h)].astype(F32) * iv[b]

    def rotated(u, b):
        return (u * cs[b] + pltpu.roll(u, 64, axis=1) * sn[b]).astype(BF)

    def last_of(b, h):
        return rb[b, h, ROWS - 1 : ROWS, :]

    def total_of(b, h):
        return last_of(b, h).astype(BF).astype(F32)

    def two_rows(above, below):
        return jnp.concatenate(
            [jnp.broadcast_to(above, (8, HEAD)), jnp.broadcast_to(below, (8, HEAD))], axis=0
        ).astype(BF)

    def states(h):
        made = []
        for b in range(2):
            normed = normed_of(b, h)
            value = normed.astype(BF)
            key = rotated(normed * gains[0, :, lanes(h)], b)
            kb[b, h] = key
            vb[b, h] = value
            shrunk = (key.astype(F32) * jnp.exp(last_of(b, h) - rb[b, h])).astype(BF)
            state = dot(shrunk, value, ((0,), (0,))).astype(BF)
            made.append(state.astype(F32))
        st[h] = made[0].astype(BF)
        early, late = total_of(0, h), total_of(1, h)
        zs[h, 0:HEAD, :] = (made[1] + jnp.exp(late) * made[0]).astype(BF)
        zs[h, HEAD : HEAD + 16, :] = two_rows(early, late)

    def pair_copy(p, came):
        return remote(
            zs.at[pl.ds(2 * p, 2)], zr.at[p if came else place], s1.at[p], r1.at[p if came else place],
            at_place(p),
        )

    def states_for(d, carry):
        p = lax.rem(place + d, QUAD)
        states(2 * p)
        states(2 * p + 1)

        @pl.when(d < QUAD)
        def _():
            pair_copy(p, False).start()

        return carry

    lax.fori_loop(1, QUAD + 1, states_for, 0)
    zr[place] = zs[pl.ds(2 * place, 2)]
    serve(1)

    def inside(h, carry):
        for b in range(2):
            query = rotated(normed_of(b, h) * gains[1, :, lanes(h)], b)
            qb[b, h] = query
            scores = dot(query, kb[b, h], ((1,), (1,)))
            spread = rb[b, h, :, 0:1] - rt[b, pl.ds(h, 1), :]
            weight = jnp.exp(jnp.where(lower, spread, -1e30))
            inner[b, h] = dot((scores * weight).astype(BF), vb[b, h])
        return carry

    lax.fori_loop(0, OWN, inside, 0)
    serve(2)

    def unless(p, own, thing):
        @pl.when(p != own)
        def _():
            thing()

    for p in range(QUAD):
        unless(p, place, lambda: pair_copy(p, True).wait_recv())

    def decay_of(p, i):
        sums = zr[p, i, HEAD : HEAD + 16, :].astype(F32)
        return sums[0:1] + sums[8:9]

    for i in range(2):
        state = zr[0, i, 0:HEAD, :].astype(F32)
        span = decay_of(0, i)
        for p in range(1, QUAD):
            now = decay_of(p, i)
            state = zr[p, i, 0:HEAD, :].astype(F32) + jnp.exp(now) * state
            span = span + now
        coarse_span = span.astype(BF).astype(F32)
        for half in range(2):
            gs[2 * i + half, 0:64, :] = state[half * 64 : half * 64 + 64].astype(BF)
            gs[2 * i + half, 64:80, :] = two_rows(coarse_span, span - coarse_span)

    def quad_copy(q, came):
        return remote(
            gs.at[q], gr.at[q if came else quad], s2.at[q], r2.at[q if came else quad], at_quad(q)
        )

    for q in range(QUAD):
        unless(q, quad, lambda: quad_copy(q, False).start())
    gr[quad] = gs[quad]
    serve(3)

    def back_copy(q, came):
        return remote(
            eo.at[q], er.at[q if came else quad], s3.at[q], r3.at[q if came else quad], at_quad(q)
        )

    state = jnp.zeros((64, HEAD), F32)
    for q in range(QUAD):
        eo[q] = state.astype(BF)
        unless(q, quad, lambda: back_copy(q, False).start())
        if q < QUAD - 1:
            unless(q, quad, lambda: quad_copy(q, True).wait_recv())
            sums = gr[q, 64:80, :].astype(F32)
            state = gr[q, 0:64, :].astype(F32) + jnp.exp(sums[0:1] + sums[8:9]) * state
    er[quad] = eo[quad]
    unless(QUAD - 1, quad, lambda: quad_copy(QUAD - 1, True).wait_recv())
    serve(4)

    def enter_copy(p, came):
        return remote(
            fo.at[p], ei.at[p if came else place], s4.at[p], r4.at[p if came else place], at_place(p)
        )

    for q in range(QUAD):
        unless(q, quad, lambda: back_copy(q, True).wait_recv())
    entry = [
        jnp.concatenate([er[2 * i], er[2 * i + 1]], axis=0).astype(F32) for i in range(2)
    ]
    for p in range(QUAD):
        for i in range(2):
            fo[p, i] = entry[i].astype(BF)
            if p < QUAD - 1:
                entry[i] = zr[p, i, 0:HEAD, :].astype(F32) + jnp.exp(decay_of(p, i)) * entry[i]
        unless(p, place, lambda: enter_copy(p, False).start())
    ei[place] = fo[place]
    serve(5)

    def head_copy(h, came):
        g = (y if came else x) * OWN + h
        return remote(act.at[g], act.at[g], as_.at[h], ar.at[h], mate)

    def finish(h, p, i):
        entering = ei[p, i]
        after = (st[h].astype(F32) + jnp.exp(total_of(0, h)) * entering.astype(F32)).astype(BF)
        for b in range(2):
            carried = dot(qb[b, h], entering if b == 0 else after)
            mixed = inner[b, h] + carried * jnp.exp(rb[b, h])
            centre = mixed - jnp.mean(mixed, axis=-1, keepdims=True)
            normal = centre * lax.rsqrt(
                jnp.mean(centre * centre, axis=-1, keepdims=True) + EPS_NORM
            )
            act[x * OWN + h, b * ROWS : (b + 1) * ROWS, :] = (
                normal * gains[2, :, lanes(h)]
            ).astype(BF)
        head_copy(h, False).start()

    def finish_of(d, carry):
        p = lax.rem(place + d, QUAD)

        @pl.when(d > 0)
        def _():
            enter_copy(p, True).wait_recv()

        for i in range(2):
            finish(2 * p + i, p, i)
        return carry

    lax.fori_loop(0, QUAD, finish_of, 0)
    serve(6)

    def partner_head(h, carry):
        head_copy(h, True).wait_recv()
        return carry

    lax.fori_loop(0, OWN, partner_head, 0)
    serve(7)

    def product(n, one, two):
        here = slice(n * COLS, (n + 1) * COLS)
        left = jnp.concatenate([act[one], act[two]], axis=1)
        right = jnp.concatenate([wz[one, :, here], wz[two, :, here]], axis=0)
        return dot(left, right)

    for n in range(PARTS):
        total = product(n, level(1), level(Z - 1))
        for d in range(2, Z // 2):
            total = total + product(n, level(d), level(Z - d))
        acc[n] = total
    serve(8)

    def out_copy(b, n):
        there = pl.ds(pl.multiple_of(x * HALF + n * COLS, COLS), COLS)
        return remote(
            ost.at[b, n], out_ref.at[:, there],
            os_.at[b, n], or_.at[x, n], {"pipe": following, "ctx": 2 * z + b},
        )

    for n in range(PARTS):
        here = slice(n * COLS, (n + 1) * COLS)
        total = acc[n] + product(n, z, level(Z // 2))
        for b in range(2):
            ost[b, n] = (
                xh[b, :, here].astype(F32) + total[b * ROWS : (b + 1) * ROWS]
            ).astype(BF)
            out_copy(b, n).start()

    for copy in first:
        copy.wait_send()
    for step in range(8):
        for k in range(SUBS):
            for way in range(2):
                if used(way, step, k):
                    ring_copy(way, step, k, 0).wait_send()
    for p in range(QUAD):
        unless(p, place, lambda: pair_copy(p, False).wait_send())
        unless(p, quad, lambda: quad_copy(p, False).wait_send())
        unless(p, quad, lambda: back_copy(p, False).wait_send())
        unless(p, place, lambda: enter_copy(p, False).wait_send())

    def head_sent(h, carry):
        head_copy(h, False).wait_send()
        return carry

    lax.fori_loop(0, OWN, head_sent, 0)
    for n in range(PARTS):
        for half in range(2):
            remote(
                ost.at[0, n], out_ref.at[:, pl.ds(half * HALF + n * COLS, COLS)],
                os_.at[0, n], or_.at[half, n], mate,
            ).wait_recv()
        for b in range(2):
            out_copy(b, n).wait_send()


def per_device(x_in, q_gain, key_gain_per_layer, out_gain, log_decay, out_weight):
    coarse, fine = (jnp.asarray(t) for t in tables())
    dma = pltpu.SemaphoreType.DMA
    vmem = pltpu.VMEM
    scratch = [
        vmem((ROWS, WIDTH), BF),
        vmem((3, 1, HALF), F32),
        vmem((HEADS, ROWS), F32),
        vmem((3, 32, HEAD), F32),
        vmem((3, ROWS, HEAD), F32),
        vmem((2, ROWS, HALF), BF),
        vmem((2, ROWS, HEAD), F32),
        vmem((2, OWN, ROWS), F32),
        vmem((2, OWN, ROWS, HEAD), F32),
        vmem((2, OWN, ROWS), F32),
        vmem((2, ROWS, HEAD), F32),
        vmem((2, ROWS, HEAD), F32),
        vmem((2, OWN, ROWS, HEAD), BF),
        vmem((2, OWN, ROWS, HEAD), BF),
        vmem((2, OWN, ROWS, HEAD), BF),
        vmem((OWN, HEAD, HEAD), BF),
        vmem((2, OWN, ROWS, HEAD), F32),
        vmem((OWN, HEAD + 16, HEAD), BF),
        vmem((QUAD, 2, HEAD + 16, HEAD), BF),
        vmem((QUAD, 80, HEAD), BF),
        vmem((QUAD, 80, HEAD), BF),
        vmem((QUAD, 64, HEAD), BF),
        vmem((QUAD, 64, HEAD), BF),
        vmem((QUAD, 2, HEAD, HEAD), BF),
        vmem((QUAD, 2, HEAD, HEAD), BF),
        vmem((Z, 128, HALF), BF),
        vmem((HEADS, 2 * ROWS, HEAD), BF),
        vmem((PARTS, 2 * ROWS, COLS), F32),
        vmem((2, PARTS, ROWS, COLS), BF),
        dma((8,)),
        dma((4,)), dma((4,)),
        dma((2, 8, SUBS)), dma((2, 8, SUBS)),
        *(dma((QUAD,)) for _ in range(8)),
        dma((OWN,)), dma((OWN,)),
        dma((2, PARTS)), dma((2, PARTS)),
    ]
    whole = pl.BlockSpec(memory_space=pltpu.VMEM)
    out = pl.pallas_call(
        kernel,
        out_shape=jax.ShapeDtypeStruct((ROWS, WIDTH), BF),
        in_specs=[pl.BlockSpec(memory_space=pltpu.HBM)] * 8,
        out_specs=whole,
        scratch_shapes=scratch,
        compiler_params=pltpu.CompilerParams(
            collective_id=0, has_side_effects=True, vmem_limit_bytes=64 * 2**20 - 2**16
        ),
        name="retention_layer",
    )(
        x_in[0, 0], q_gain, key_gain_per_layer, out_gain, log_decay[0].T, out_weight[0], coarse, fine
    )
    return out[None, None]


def solution(mesh):
    placed = (
        P("pipe", None, "ctx", None),
        P("pipe", None),
        P("pipe", None),
        P("pipe", None),
        P("pipe", "ctx", None),
        P("pipe", "ctx", None),
    )
    return jax.shard_map(
        per_device,
        mesh=mesh,
        in_specs=placed,
        out_specs=P("pipe", None, "ctx", None),
        check_vma=False,
    )
```

time: 114 us -> 104 us (0.912)
  local copies, waits for them, and re-layouts: 7.42 us -> 1.98 us
  Pallas kernels: 106 us -> 101 us
    unnamed x17 -> x1, local copies, waits for them, and re-layouts: 7.42 us -> 1.98 us
    pallas_call x1, Pallas kernels: 106 us -> 101 us  [per_device(): pl.pallas_call(kernel, out_shape=jax.ShapeDtypeStruct((ROWS, WIDTH), BF),...]
where the time goes in v2:
time: 104 us; the launch traced here: 103 us
  Pallas kernels  101 us (97%)
  local copies, waits for them, and re-layouts  1.98 us (2%)
    pallas_call x1, Pallas kernels, per_device(): pl.pallas_call(kernel, out_shape=jax.ShapeDtypeStruct((ROWS, WIDTH), BF),...  101 us

profile of v2, /device:TPU:2, one launch (start us, length us, event | category | flops | bytes accessed | tf_op | source)
XLA Modules:
  0.0 103.4 jit_solution(5371885567428851882)
XLA Ops:
  0.0 101.4 %retention_layer.1 = bf16[160,2048]{1,0:T(8,128)(2,1)} custom-call(bf16[160,2048]{1,0:T(8,128)(2,1)} %bitcast.7, f32[1,2048]{1,0:T(1,128)} %qg_hbm.1, f32[1,2048]{1,0:T(1,128)} %kg_hbm.1, f32[1,2048]{1,0:T(1,128)} %og_hbm.1, f32[16,160]{1,0:T(8,128)} %bitcast.9, bf16[64,2048]{1,0:T(8,128)(2,1)} %bitcast.8, f32[3,32,128]{2,1,0:T(8,128)} %constant.4.clone.coarse_hbm, ...), custom_call_target="tpu_custom_call" | custom-call | tf_op jit(solution)/shard_map/retention_layer/pallas_call | solution.py:440
  101.5 2.0 %copy.10 = bf16[1,1,160,2048]{3,2,1,0:T(8,128)(2,1)} copy(bf16[1,1,160,2048]{3,2,1,0:T(8,128)(2,1)} %bitcast.6) | data formatting | bytes 1310720

commit v3 on v2

--- a/solution.py
+++ b/solution.py
@@ -40,7 +40,7 @@
     x_hbm, qg_hbm, kg_hbm, og_hbm, ld_hbm, w_hbm, coarse_hbm, fine_hbm,
     out_ref,
     xv, gains, ldv, coarse, fine,
-    xh, iv, ldh, rb, rt, cs, sn, kb, vb, qb, st, inner, zs, zr, gs, gr, eo, er, fo, ei, wz, act, acc, ost,
+    xh, iv, sm, ldh, rb, rt, cs, sn, kb, vb, qb, st, inner, zs, zr, gs, gr, eo, er, fo, ei, wz, act, acc, ost,
     ins, is_, ir, ws, wr, s1, r1, s2, r2, s3, r3, s4, r4, as_, ar, os_, or_,
 ):
     pipe, ctx = lax.axis_index("pipe"), lax.axis_index("ctx")
@@ -94,8 +94,18 @@
     scale = lax.rsqrt(jnp.mean(floats * floats, axis=-1, keepdims=True) + EPS_RMS)
     iv[x] = jnp.broadcast_to(scale, (ROWS, HEAD))
     xh[x] = xv[:, mine]
+    rows_i = lax.broadcasted_iota(jnp.int32, (ROWS, ROWS), 0)
+    cols_i = lax.broadcasted_iota(jnp.int32, (ROWS, ROWS), 1)
+    lower = rows_i >= cols_i
+    lower_f = lower.astype(F32)
+    same = rows_i == cols_i
+    exact = lax.Precision.HIGHEST
+    sm[OWN : 2 * OWN, :] = dot(
+        jnp.ones((8, ROWS), F32), jnp.where(same, scale, 0.0), precision=exact
+    )
     fetches[2].wait()
-    ldh[x] = ldv[pl.ds(pl.multiple_of(x * OWN, OWN), OWN), :]
+    ldh[x, 0:OWN, :] = ldv[pl.ds(pl.multiple_of(x * OWN, OWN), OWN), :]
+    sm[0:OWN, :] = ldv[pl.ds(pl.multiple_of(y * OWN, OWN), OWN), :]
     fetches[0].wait()
 
     pl.semaphore_wait(barrier, len(greeted))
@@ -121,11 +131,8 @@
 
     first = [
         remote(w_hbm.at[:, theirs], wz.at[z, own_rows], is_.at[0], ir.at[0], mate),
-        remote(
-            ldv.at[pl.ds(pl.multiple_of(y * OWN, OWN), OWN)], ldh.at[x], is_.at[1], ir.at[1], mate
-        ),
-        remote(iv.at[x], iv.at[x], is_.at[2], ir.at[2], mate),
-        remote(xv.at[:, theirs], xh.at[x], is_.at[3], ir.at[3], mate),
+        remote(sm, ldh.at[x], is_.at[1], ir.at[1], mate),
+        remote(xv.at[:, theirs], xh.at[x], is_.at[2], ir.at[2], mate),
     ]
     first[0].start()
     serve(0, (0, 1))
@@ -139,24 +146,15 @@
         ca, sa, su = coarse[0, row], coarse[1, row], coarse[2, row]
         cs[b] = ca * fine[0] - su * fine[2]
         sn[b] = sa * fine[0] + ca * fine[1]
-    rows_i = lax.broadcasted_iota(jnp.int32, (ROWS, ROWS), 0)
-    cols_i = lax.broadcasted_iota(jnp.int32, (ROWS, ROWS), 1)
-    lower = rows_i >= cols_i
-    lower_f = lower.astype(F32)
     for i in (5, 6, 7):
         fetches[i].wait()
 
-    first[0].wait_recv()
-    serve(0, (2, 3))
-    first[1].wait_recv()
-    for b in range(2):
-        lds = ldh[b]
-        rt[b] = dot(lds, lower_f, ((1,), (1,)), lax.Precision.HIGHEST)
-        run = dot(lower_f, lds, ((1,), (1,)), lax.Precision.HIGHEST)
+    def sums_of(b):
+        lds = ldh[b, 0:OWN, :]
+        rt[b] = dot(lds, lower_f, ((1,), (1,)), exact)
+        run = dot(lower_f, lds, ((1,), (1,)), exact)
         for h in range(OWN):
             rb[b, h] = jnp.broadcast_to(run[:, h : h + 1], (ROWS, HEAD))
-    first[2].wait_recv()
-    first[3].wait_recv()
 
     def lanes(h):
         return pl.ds(pl.multiple_of(h * HEAD, HEAD), HEAD)
@@ -178,21 +176,45 @@
             [jnp.broadcast_to(above, (8, HEAD)), jnp.broadcast_to(below, (8, HEAD))], axis=0
         ).astype(BF)
 
-    def states(h):
-        made = []
-        for b in range(2):
-            normed = normed_of(b, h)
-            value = normed.astype(BF)
-            key = rotated(normed * gains[0, :, lanes(h)], b)
-            kb[b, h] = key
-            vb[b, h] = value
-            shrunk = (key.astype(F32) * jnp.exp(last_of(b, h) - rb[b, h])).astype(BF)
-            state = dot(shrunk, value, ((0,), (0,))).astype(BF)
-            made.append(state.astype(F32))
-        st[h] = made[0].astype(BF)
-        early, late = total_of(0, h), total_of(1, h)
-        zs[h, 0:HEAD, :] = (made[1] + jnp.exp(late) * made[0]).astype(BF)
-        zs[h, HEAD : HEAD + 16, :] = two_rows(early, late)
+    def states(b, h):
+        normed = normed_of(b, h)
+        value = normed.astype(BF)
+        key = rotated(normed * gains[0, :, lanes(h)], b)
+        kb[b, h] = key
+        vb[b, h] = value
+        shrunk = (key.astype(F32) * jnp.exp(last_of(b, h) - rb[b, h])).astype(BF)
+        st[b, h] = dot(shrunk, value, ((0,), (0,))).astype(BF)
+
+    def inside(b, h):
+        query = rotated(normed_of(b, h) * gains[1, :, lanes(h)], b)
+        qb[b, h] = query
+        scores = dot(query, kb[b, h], ((1,), (1,)))
+        spread = rb[b, h, :, 0:1] - rt[b, pl.ds(h, 1), :]
+        weight = jnp.exp(jnp.where(lower, spread, -1e30))
+        inner[b, h] = dot((scores * weight).astype(BF), vb[b, h])
+
+    def over_heads(thing, b, start, stop):
+        def step(i, carry):
+            thing(b, 2 * i)
+            thing(b, 2 * i + 1)
+            return carry
+
+        lax.fori_loop(start // 2, stop // 2, step, 0)
+
+    sums_of(x)
+    over_heads(states, x, 0, OWN)
+    first[0].wait_recv()
+    serve(0, (2, 3))
+    over_heads(inside, x, 0, OWN // 2)
+    serve(1, (0, 1))
+    over_heads(inside, x, OWN // 2, OWN)
+    first[1].wait_recv()
+    sums_of(y)
+    iv[y] = dot(
+        jnp.where(same, ldh[y, OWN : OWN + 1, :], 0.0), jnp.ones((ROWS, HEAD), F32), precision=exact
+    )
+    serve(1, (2, 3))
+    first[2].wait_recv()
 
     def pair_copy(p, came):
         return remote(
@@ -200,10 +222,18 @@
             at_place(p),
         )
 
+    def pair_states(h):
+        states(y, h)
+        early, late = total_of(0, h), total_of(1, h)
+        zs[h, 0:HEAD, :] = (
+            st[1, h].astype(F32) + jnp.exp(late) * st[0, h].astype(F32)
+        ).astype(BF)
+        zs[h, HEAD : HEAD + 16, :] = two_rows(early, late)
+
     def states_for(d, carry):
         p = lax.rem(place + d, QUAD)
-        states(2 * p)
-        states(2 * p + 1)
+        pair_states(2 * p)
+        pair_states(2 * p + 1)
 
         @pl.when(d < QUAD)
         def _():
@@ -213,20 +243,10 @@
 
     lax.fori_loop(1, QUAD + 1, states_for, 0)
     zr[place] = zs[pl.ds(2 * place, 2)]
-    serve(1)
-
-    def inside(h, carry):
-        for b in range(2):
-            query = rotated(normed_of(b, h) * gains[1, :, lanes(h)], b)
-            qb[b, h] = query
-            scores = dot(query, kb[b, h], ((1,), (1,)))
-            spread = rb[b, h, :, 0:1] - rt[b, pl.ds(h, 1), :]
-            weight = jnp.exp(jnp.where(lower, spread, -1e30))
-            inner[b, h] = dot((scores * weight).astype(BF), vb[b, h])
-        return carry
-
-    lax.fori_loop(0, OWN, inside, 0)
-    serve(2)
+    serve(2, (0, 1))
+    over_heads(inside, y, 0, OWN // 2)
+    serve(2, (2, 3))
+    over_heads(inside, y, OWN // 2, OWN)
 
     def unless(p, own, thing):
         @pl.when(p != own)
@@ -304,7 +324,7 @@
 
     def finish(h, p, i):
         entering = ei[p, i]
-        after = (st[h].astype(F32) + jnp.exp(total_of(0, h)) * entering.astype(F32)).astype(BF)
+        after = (st[0, h].astype(F32) + jnp.exp(total_of(0, h)) * entering.astype(F32)).astype(BF)
         for b in range(2):
             carried = dot(qb[b, h], entering if b == 0 else after)
             mixed = inner[b, h] + carried * jnp.exp(rb[b, h])
@@ -335,8 +355,8 @@
         head_copy(h, True).wait_recv()
         return carry
 
+    serve(7)
     lax.fori_loop(0, OWN, partner_head, 0)
-    serve(7)
 
     def product(n, one, two):
         here = slice(n * COLS, (n + 1) * COLS)
@@ -407,7 +427,8 @@
         vmem((3, ROWS, HEAD), F32),
         vmem((2, ROWS, HALF), BF),
         vmem((2, ROWS, HEAD), F32),
-        vmem((2, OWN, ROWS), F32),
+        vmem((2 * OWN, ROWS), F32),
+        vmem((2, 2 * OWN, ROWS), F32),
         vmem((2, OWN, ROWS, HEAD), F32),
         vmem((2, OWN, ROWS), F32),
         vmem((2, ROWS, HEAD), F32),
@@ -415,7 +436,7 @@
         vmem((2, OWN, ROWS, HEAD), BF),
         vmem((2, OWN, ROWS, HEAD), BF),
         vmem((2, OWN, ROWS, HEAD), BF),
-        vmem((OWN, HEAD, HEAD), BF),
+        vmem((2, OWN, HEAD, HEAD), BF),
         vmem((2, OWN, ROWS, HEAD), F32),
         vmem((OWN, HEAD + 16, HEAD), BF),
         vmem((QUAD, 2, HEAD + 16, HEAD), BF),
@@ -430,18 +451,17 @@
         vmem((PARTS, 2 * ROWS, COLS), F32),
         vmem((2, PARTS, ROWS, COLS), BF),
         dma((8,)),
-        dma((4,)), dma((4,)),
+        dma((3,)), dma((3,)),
         dma((2, 8, SUBS)), dma((2, 8, SUBS)),
         *(dma((QUAD,)) for _ in range(8)),
         dma((OWN,)), dma((OWN,)),
         dma((2, PARTS)), dma((2, PARTS)),
     ]
-    whole = pl.BlockSpec(memory_space=pltpu.VMEM)
     out = pl.pallas_call(
         kernel,
         out_shape=jax.ShapeDtypeStruct((ROWS, WIDTH), BF),
         in_specs=[pl.BlockSpec(memory_space=pltpu.HBM)] * 8,
-        out_specs=whole,
+        out_specs=pl.BlockSpec(memory_space=pltpu.HBM),
         scratch_shapes=scratch,
         compiler_params=pltpu.CompilerParams(
             collective_id=0, has_side_effects=True, vmem_limit_bytes=64 * 2**20 - 2**16

time: 104 us -> 93.6 us (0.90)
  the two profiles are of different devices: /device:TPU:2 before, /device:TPU:32 now
where the time goes in v3:
time: 93.6 us; the launch traced here: 93.4 us
  Pallas kernels  91.4 us (98%)
  local copies, waits for them, and re-layouts  1.98 us (2%)
    pallas_call x1, Pallas kernels, per_device(): pl.pallas_call(kernel, out_shape=jax.ShapeDtypeStruct((ROWS, WIDTH), BF),...  91.4 us
    unnamed x1, local copies, waits for them, and re-layouts  1.98 us

profile of v3, /device:TPU:32, one launch (start us, length us, event | category | flops | bytes accessed | tf_op | source)
XLA Modules:
  0.0 93.4 jit_solution(13659725271361548191)
XLA Ops:
  0.0 91.4 %retention_layer.1 = bf16[160,2048]{1,0:T(8,128)(2,1)} custom-call(bf16[160,2048]{1,0:T(8,128)(2,1)} %bitcast.7, f32[1,2048]{1,0:T(1,128)} %qg_hbm.1, f32[1,2048]{1,0:T(1,128)} %kg_hbm.1, f32[1,2048]{1,0:T(1,128)} %og_hbm.1, f32[16,160]{1,0:T(8,128)} %bitcast.9, bf16[64,2048]{1,0:T(8,128)(2,1)} %bitcast.8, f32[3,32,128]{2,1,0:T(8,128)} %constant.4.clone.coarse_hbm, ...), custom_call_target="tpu_custom_call" | custom-call | tf_op jit(solution)/shard_map/retention_layer/pallas_call | solution.py:460
  91.4 2.0 %copy.10 = bf16[1,1,160,2048]{3,2,1,0:T(8,128)(2,1)} copy(bf16[1,1,160,2048]{3,2,1,0:T(8,128)(2,1)} %bitcast.6) | data formatting | bytes 1310720
